TPU v7x, 768 devices: a whole 4x8x12 slice. The times are simulated.
768 devices in a mesh: grp: 16 (over y, core), dom: 48 (over z, x).
Axes of the slice: x: 4, y: 8, z: 12, core: 2. Of those that a mesh axis runs over, the one named last changes fastest.
Arguments:
- a_tiles: bfloat16 [3072, 8, 128, 128], P(('grp', 'dom')), may hold values from -0.1875 to 0.1875
- a_cols: int32 [3072, 8], P(('grp', 'dom')), may hold values from 0 to 12, as said below
- p_tiles: bfloat16 [3072, 128, 128], P(('grp', 'dom')), may hold values from -0.47851562 to 0.47851562
- send_list: int32 [768, 8], P(('grp', 'dom')), may hold values from 0 to 3
- term_slot: int32 [3072, 4, 8, 4], P(('grp', 'dom')), may hold values from 0 to 63
- owner_slot: int32 [49152], P(('grp', 'dom')), may hold values from 0 to 12287, as said below
Outputs:
- coarse: float32 [12288, 1024], P('dom')
Inputs may be any that keep to these rules, and one draw needn't show every extreme that they name: `a_cols`: entries below 4 name local blocks; 4 + i names the i-th block received from the lower neighbour, 8 + i the i-th from the higher one, 12 the zero block. Every block row's first tile is local. The first device never names the lower neighbour's blocks and the last never the higher one's; every other device names some block of its lower neighbour and some block of its higher neighbour. `owner_slot`: an entry c names the coarse block owned by the device with dom index c // 256 and grp index (c // 16) % 16, the same grp index as the device that holds the entry. Of one device's 64 entries, at most 2 name blocks of any one owner, and exactly 2 do for some owner.
All inputs are finite; a program needn't handle non-finite values.
Results may differ from a plain program's by a relative error of at most 0.0029.
Values may be sent and summed in bfloat16 or wider, within the bound.
No kernel may reach another device: no remote copies, remote signals or barrier semaphores. Data moves between devices by JAX's collectives and lax.ppermute only.
A program may use at most 64 MiB of HBM per device.

v0:
```python
import jax
import jax.numpy as jnp
from jax import lax
from jax.sharding import PartitionSpec as P

KA = 8
LP = 64
OS = 16


def with_halo(x, sides, width):
    for axis, dim in sides:
        size, length = (lax.axis_size(axis), x.shape[dim])
        up = [(i, (i + 1) % size) for i in range(size - 1)]
        down = [(j, i) for i, j in up]
        last = lax.slice_in_dim(x, length - width, length, axis=dim)
        leading = lax.slice_in_dim(x, 0, width, axis=dim)
        before = lax.ppermute(last, axis, up)
        after = lax.ppermute(leading, axis, down)
        x = jnp.concatenate([before, x, after], axis=dim)
    return x


def body(a_tiles, a_cols, p_tiles, send_list, term_slot, owner_slot):
    blocks = a_tiles.shape[0]
    rows = p_tiles.shape[1]
    kp_count = term_slot.shape[1]
    columns = p_tiles.shape[2]
    coarse_width = columns // kp_count
    side = send_list.shape[1] // 2
    outgoing = p_tiles[send_list[0]]
    arrived = with_halo(outgoing, ((("grp", "dom"), 0),), side)
    zero_block = jnp.zeros((1, rows, columns), p_tiles.dtype)
    table = jnp.concatenate([p_tiles, arrived[:side], arrived[3 * side :], zero_block], 0)
    gathered = table[a_cols]
    product = jnp.einsum(
        "nark,nakc->nrac", a_tiles, gathered, preferred_element_type=jnp.float32
    ).astype(jnp.bfloat16)
    mine = p_tiles.reshape(blocks, rows, kp_count, coarse_width)
    terms = jnp.einsum(
        "nrqx,nrapy->nqapxy",
        mine,
        product.reshape(blocks, rows, KA, kp_count, coarse_width),
        preferred_element_type=jnp.float32,
    )
    terms = terms.reshape(-1, coarse_width * coarse_width)
    slots = term_slot.reshape(-1)
    select = (slots[None, :] == jnp.arange(LP)[:, None]).astype(jnp.float32)
    partial_value = jnp.dot(select, terms, precision=lax.Precision.HIGHEST)
    dom_count = lax.axis_size("dom")
    grp_count = lax.axis_size("grp")
    owner_dom = owner_slot // (grp_count * OS)
    within = owner_slot % OS
    target = owner_dom * OS + within
    placing = (target[None, :] == jnp.arange(dom_count * OS)[:, None]).astype(jnp.float32)
    dense_table = jnp.dot(placing, partial_value, precision=lax.Precision.HIGHEST)
    owned = lax.psum_scatter(dense_table, "dom", scatter_dimension=0, tiled=True)
    return lax.all_gather(owned, "grp", axis=0, tiled=True)


def solution(mesh):
    placed = (
        P(("grp", "dom"), None, None, None),
        P(("grp", "dom"), None),
        P(("grp", "dom"), None, None),
        P(("grp", "dom"), None),
        P(("grp", "dom"), None, None, None),
        P(("grp", "dom")),
    )
    return jax.shard_map(
        body, mesh=mesh, in_specs=placed, out_specs=P("dom", None), check_vma=False
    )
```

profile of v0, /device:TPU:1, one launch (start us, length us, event | category | flops | bytes accessed | tf_op | source)
XLA Modules:
  0.0 541.5 jit_solution(16604580512517740866)
XLA Ops:
  6.5 0.0 copy-start
  6.5 0.0 reduce-scatter.2.cloned.1.call-start
  6.5 0.7 fusion.5
  7.3 1.5 gather_fusion
  8.8 3.9 collective-permute-start
  12.8 15.9 %collective-permute-start.1 = (bf16[4,128,128]{2,1,0:T(8,128)(2,1)S(1)}, bf16[4,128,128]{2,1,0:T(8,128)(2,1)S(1)}, u32[]{:S(2)}, u32[]{:S(2)}) collective-permute-start(bf16[4,128,128]{2,1,0:T(8,128)(2,1)S(1)} %get-tuple-element.6), channel_id=1, source_target_pairs={{1,0},{2,1},{3,2},{4,3},{5,4},{6,5},{7,6},{8,7},{9,8},{10,9},{11,1... | collective-permute-start | bytes 393224 | tf_op jit(solution)/shard_map/ppermute | solution.py:19
  28.7 0.7 compare_select_fusion
  29.3 0.7 fusion.4
  30.0 1.0 copy.11
  31.0 0.1 reshape.52
  31.1 0.9 copy.9
  32.0 0.1 eq.33
  32.1 0.1 pad.3.clone
  32.2 0.0 collective-permute-done
  32.2 0.0 collective-permute-done.1
  32.3 1.0 maximum_maximum_fusion
  33.3 0.7 gather_fusion.1
  34.0 0.0 copy-done
  34.0 0.9 convolution_convert_fusion
  34.9 4.5 convolution_bitcast_fusion
  39.4 8.7 %copy.12 = f32[4,4,8,4,32,32]{5,4,3,2,1,0:T(8,128)} copy(f32[4,4,8,4,32,32]{4,5,1,3,2,0:T(8,128)} %convolution_bitcast_fusion) | data formatting | bytes 4194304 | tf_op jit(solution)/shard_map/nrqx,nrapy->nqapxy/transpose | solution.py:40
  48.1 6.6 %reshape.41 = f32[512,1024]{1,0:T(8,128)S(1)} reshape(f32[4,4,8,4,32,32]{5,4,3,2,1,0:T(8,128)} %copy.12) | data formatting | bytes 4194304 | tf_op jit(solution)/shard_map/reshape | solution.py:46
  54.7 0.9 fusion.2
  55.6 3.0 fusion
  58.7 0.0 reduce-scatter.2.cloned.1.call-update
  58.7 0.0 all-gather.2.cloned.1.call-start
  58.8 421.6 %reduce-scatter.2.cloned.1.call-done = f32[16,1024]{1,0:T(8,128)} async-done(((f32[768,1024]{1,0:T(8,128)}), f32[16,1024]{1,0:T(8,128)}) %reduce-scatter.2.cloned.1.call-update) | async-done | bytes 65552 | tf_op jit(solution)/shard_map/reduce_scatter | solution.py:57
  480.4 0.0 all-gather.2.cloned.1.call-update
  480.4 51.9 %all-gather.2.cloned.1.call-done = f32[256,1024]{1,0:T(8,128)} async-done(((f32[16,1024]{1,0:T(8,128)}), f32[256,1024]{1,0:T(8,128)}) %all-gather.2.cloned.1.call-update) | async-done | bytes 1048592 | tf_op jit(solution)/shard_map/all_gather | solution.py:58
  532.3 2.3 copy.17
  (3 shorter events, 0.0 us)
Async XLA Ops:
  6.5 27.5 %copy-start = (bf16[4,8,128,128]{3,2,1,0:T(8,128)(2,1)S(1)}, bf16[4,8,128,128]{3,2,1,0:T(8,128)(2,1)}, u32[]{:S(2)}) copy-start(bf16[4,8,128,128]{3,2,1,0:T(8,128)(2,1)} %param.6) | copy-start | bytes 3145732
  6.5 473.9 %reduce-scatter.2.cloned.1.call-start = ((), (), s32[]{:S(2)}) async-start(), calls=%async_computation.1 | async-start | bytes 3211264 | tf_op jit(solution)/shard_map/reduce_scatter | solution.py:57
  8.8 23.4 %collective-permute-start = (bf16[4,128,128]{2,1,0:T(8,128)(2,1)S(1)}, bf16[4,128,128]{2,1,0:T(8,128)(2,1)S(1)}, u32[]{:S(2)}, u32[]{:S(2)}) collective-permute-start(bf16[4,128,128]{2,1,0:T(8,128)(2,1)S(1)} %get-tuple-element.5), channel_id=1, source_target_pairs={{0,1},{1,2},{2,3},{3,4},{4,5},{5,6},{6,7},{7,8},{8,9},{9,10},{10,1... | collective-permute-start | bytes 393224 | tf_op jit(solution)/shard_map/ppermute | solution.py:18
  12.8 19.5 %collective-permute-start.1 = (bf16[4,128,128]{2,1,0:T(8,128)(2,1)S(1)}, bf16[4,128,128]{2,1,0:T(8,128)(2,1)S(1)}, u32[]{:S(2)}, u32[]{:S(2)}) collective-permute-start(bf16[4,128,128]{2,1,0:T(8,128)(2,1)S(1)} %get-tuple-element.6), channel_id=1, source_target_pairs={{1,0},{2,1},{3,2},{4,3},{5,4},{6,5},{7,6},{8,7},{9,8},{10,9},{11,1... | collective-permute-start | bytes 393224 | tf_op jit(solution)/shard_map/ppermute | solution.py:19
  58.7 473.6 %all-gather.2.cloned.1.call-start = ((), (), s32[]{:S(2)}) async-start(), calls=%async_computation.2 | async-start | bytes 1114112 | tf_op jit(solution)/shard_map/all_gather | solution.py:58
Sparse Core Ops, SparseCore 0:
  58.8 421.5 reduce-scatter.1
  482.8 49.5 all-gather.1
where the time goes:
time: 542 us; the launch traced here: 541 us
  waiting for transfers between devices  474 us (87%)
  local copies, waits for them, and re-layouts  22.1 us (4%)
  starting transfers between devices  19.9 us (4%)
  between operations  13.5 us (2%)
  matrix products  9.36 us (2%)
    reduce_scatter x1, waiting for transfers between devices, body(): lax.psum_scatter(dense_table, 'dom', scatter_dimension=0, tiled=True)  422 us
    all_gather x1, waiting for transfers between devices, body(): return lax.all_gather(owned, 'grp', axis=0, tiled=True)  51.9 us
    ppermute x1, starting transfers between devices, with_halo(): after = lax.ppermute(leading, axis, down)  15.9 us
  transfers between devices with their start and end apart: 4, of which 2 were waited for; matrix products, arithmetic and copies ran while one was open for 1% of the time, Pallas kernels for 0%

commit v1 on v0

v1 whole, which is shorter than its diff:
```python
import jax
import jax.numpy as jnp
from jax import lax
from jax.experimental import pallas as pl
from jax.experimental.pallas import tpu as pltpu
from jax.sharding import PartitionSpec as P

KA = 8
KP = 4
NB = 4
CW = 32
B = 128
LP = 64
OS = 16
CAP = 2
META = 128
SMALL = 4 * 1024 * 1024
MEDIUM = 16 * 1024 * 1024
PICK_GRANT = 60 * 1024 * 1024
VMEM = pltpu.VMEM
SMEM = pltpu.SMEM


def is_odd():
    return lax.rem(lax.axis_index("dom"), 2)


def pick_kernel(send_ref, p_ref, far_ref, near_ref):
    to_far = NB * is_odd()
    to_near = NB - to_far
    for k in range(NB):
        near_ref[k] = p_ref[send_ref[0, to_near + k]]
        far_ref[k] = p_ref[send_ref[0, to_far + k]]


def pick(send_list, p_tiles):
    shape = jax.ShapeDtypeStruct(p_tiles.shape, p_tiles.dtype)
    return pl.pallas_call(
        pick_kernel,
        out_shape=(shape, shape),
        in_specs=[pl.BlockSpec(memory_space=SMEM), pl.BlockSpec(memory_space=VMEM)],
        out_specs=(pl.BlockSpec(memory_space=VMEM),) * 2,
        compiler_params=pltpu.CompilerParams(vmem_limit_bytes=PICK_GRANT),
    )(send_list, p_tiles)


def lane_turn(v):
    lane = lax.broadcasted_iota(jnp.int32, (8, B), 1)
    low = lane < 64
    even = (lane % 64) < 32

    def swap(a, b, mask, shift):
        moved = pltpu.roll(jnp.where(mask, b, a), shift, 1)
        return jnp.where(mask, a, moved), jnp.where(mask, moved, b)

    def swap_near(a, b):
        first = jnp.where(even, a, pltpu.roll(b, 32, 1))
        second = jnp.where(even, pltpu.roll(a, 96, 1), b)
        return first, second

    v0, v2 = swap(v[0], v[2], low, 64)
    v1, v3 = swap(v[1], v[3], low, 64)
    v0, v1 = swap_near(v0, v1)
    v2, v3 = swap_near(v2, v3)
    return v0, v1, v2, v3


def add_terms(accs, places, terms):
    rows = [pl.ds(pl.multiple_of(place * 8, 8), 8) for place in places]
    sums = [acc[at, :] + term for acc, at, term in zip(accs, rows, terms)]
    for acc, at, value in zip(accs, rows, sums):
        acc[at, :] = value


def terms_kernel(cols_ref, slots_ref, pos_ref, meta_ref, a_ref, p_ref, far_ref, near_ref, out_ref, table, product, *accs):
    table[0:4] = p_ref[...]
    odd = is_odd()
    table[pl.ds(2 * NB - NB * odd, NB)] = near_ref[...]
    table[pl.ds(NB + NB * odd, NB)] = far_ref[...]
    table[3 * NB] = jnp.zeros((B, B), jnp.bfloat16)
    for acc in accs:
        acc[...] = jnp.zeros_like(acc)
    row = lax.broadcasted_iota(jnp.int32, (B, B), 0)
    column = lax.broadcasted_iota(jnp.int32, (B, B), 1)
    source = (row // 32) * 32 + 4 * (row % 8) + (row % 32) // 8
    turn = (column == source).astype(jnp.bfloat16)
    for n in range(NB):
        turned = lax.dot_general(turn, p_ref[n], (((1,), (1,)), ((), ())), preferred_element_type=jnp.float32).astype(jnp.bfloat16)
        for a in range(KA):
            product[n, :, a * B : (a + 1) * B] = jnp.dot(
                a_ref[n, a], table[cols_ref[n, a]], preferred_element_type=jnp.float32
            ).astype(jnp.bfloat16)
        for a in range(0, KA, 2):
            tiles = jnp.dot(turned, product[n, :, a * B : (a + 2) * B], preferred_element_type=jnp.float32)
            for half in range(2):
                tile = tiles[:, half * B : (half + 1) * B]
                for q in range(KP):
                    v = [tile[q * 32 + 8 * j : q * 32 + 8 * j + 8] for j in range(4)]
                    first = ((n * KP + q) * KA + a + half) * KP
                    add_terms(accs, [pos_ref[slots_ref[first + p]] for p in range(KP)], lane_turn(v))
    count = out_ref.shape[0]
    for i in range(8):
        parts = [acc[pl.ds(i, count, stride=8), :] for acc in accs]
        total = (parts[0] + parts[1]) + (parts[2] + parts[3])
        out_ref[:, i * B : (i + 1) * B] = total.astype(jnp.bfloat16)
    out_ref[:, 8 * B :] = meta_ref[...]


def send_blocks(a_cols, slots, pos, meta, a_tiles, p_tiles, far, near):
    count = meta.shape[0]
    vmem = pl.BlockSpec(memory_space=VMEM)
    smem = pl.BlockSpec(memory_space=SMEM)
    return pl.pallas_call(
        terms_kernel,
        out_shape=jax.ShapeDtypeStruct((count, 8 * B + META), jnp.bfloat16),
        in_specs=[smem, smem, smem, vmem, vmem, vmem, vmem, vmem],
        out_specs=vmem,
        scratch_shapes=[
            VMEM((3 * NB + 1, B, B), jnp.bfloat16),
            VMEM((NB, B, KA * B), jnp.bfloat16),
        ]
        + [VMEM((count * 8, B), jnp.float32)] * KP,
        compiler_params=pltpu.CompilerParams(vmem_limit_bytes=MEDIUM),
        cost_estimate=pl.CostEstimate(flops=300_000_000, bytes_accessed=2_000_000, transcendentals=0),
    )(a_cols, slots, pos, meta, a_tiles, p_tiles, far, near)


def owner_kernel(in_ref, out_ref):
    within = in_ref[:, 8 * B :].astype(jnp.float32)
    lane = lax.broadcasted_iota(jnp.int32, within.shape, 1).astype(jnp.float32)
    place = jnp.where(within == lane, 1.0, 0.0).T[:OS].astype(jnp.bfloat16)
    out_ref[...] = jnp.dot(place, in_ref[:, : 8 * B], preferred_element_type=jnp.float32).astype(jnp.bfloat16)


def own_sum(received):
    return pl.pallas_call(
        owner_kernel,
        out_shape=jax.ShapeDtypeStruct((OS, 8 * B), jnp.bfloat16),
        in_specs=[pl.BlockSpec(memory_space=VMEM)],
        out_specs=pl.BlockSpec(memory_space=VMEM),
        compiler_params=pltpu.CompilerParams(vmem_limit_bytes=SMALL),
    )(received)


def body(a_tiles, a_cols, p_tiles, send_list, term_slot, owner_slot):
    dom_count = lax.axis_size("dom")
    grp_count = lax.axis_size("grp")
    devices = dom_count * grp_count
    to_far, to_near = pick(send_list, p_tiles)
    near = [(i, i ^ 1) for i in range(devices)]
    far = [(i, ((i + 1) ^ 1) - 1) for i in range(1, devices - 1)]
    from_far = lax.ppermute(to_far, ("grp", "dom"), far)
    from_near = lax.ppermute(to_near, ("grp", "dom"), near)

    rows = dom_count * CAP
    owner = owner_slot // (grp_count * OS)
    within = owner_slot % OS
    index = jnp.arange(LP)
    same = (owner[:, None] == owner[None, :]) & (index[None, :] < index[:, None])
    pos = owner * CAP + jnp.sum(same.astype(jnp.int32), axis=1)
    here = pos[None, :] == jnp.arange(rows)[:, None]
    meta = jnp.sum(jnp.where(here, within[None, :], 0), axis=1).astype(jnp.bfloat16)
    meta = jnp.broadcast_to(meta[:, None], (rows, META))

    blocks = send_blocks(a_cols, term_slot.reshape(-1), pos, meta, a_tiles, p_tiles, from_far, from_near)
    received = lax.all_to_all(blocks, "dom", 0, 0, tiled=True)
    owned = own_sum(received)
    return lax.all_gather(owned, "grp", axis=0, tiled=True).astype(jnp.float32)


def solution(mesh):
    placed = (
        P(("grp", "dom"), None, None, None),
        P(("grp", "dom"), None),
        P(("grp", "dom"), None, None),
        P(("grp", "dom"), None),
        P(("grp", "dom"), None, None, None),
        P(("grp", "dom")),
    )
    return jax.shard_map(
        body, mesh=mesh, in_specs=placed, out_specs=P("dom", None), check_vma=False
    )
```

time: 542 us -> 72 us (0.13)
  waiting for transfers between devices: 474 us -> 3.37 us
  blocking collectives: 0 us -> 40.7 us
  local copies, waits for them, and re-layouts: 22.1 us -> 1.75 us
  between operations: 13.5 us -> 0.1 us
  matrix products: 9.36 us -> 0 us
    reduce_scatter x1 -> x0, waiting for transfers between devices: 422 us -> none  [body(): lax.psum_scatter(dense_table, 'dom', scatter_dimension=0, tiled=True)]
    all_gather x1 -> x0, waiting for transfers between devices: 51.9 us -> none  [body(): return lax.all_gather(owned, 'grp', axis=0, tiled=True)]
    all_gather x0 -> x1, blocking collectives: none -> 20.8 us  [body(): return lax.all_gather(owned, 'grp', axis=0, tiled=True).astype(jnp.float32)]
    all_to_all x0 -> x1, blocking collectives: none -> 19.9 us  [body(): received = lax.all_to_all(blocks, 'dom', 0, 0, tiled=True)]
    dot_general x4 -> x0, matrix products: 9.36 us -> none  [the longest x1 4.51 us: body(): jnp.einsum('nrqx,nrapy->nqapxy', mine, product.reshape(blocks, rows, KA,...]
    transpose x1 -> x0, local copies, waits for them, and re-layouts: 8.65 us -> none  [body(): jnp.einsum('nrqx,nrapy->nqapxy', mine, product.reshape(blocks, rows, KA,...]
    reshape x1, local copies, waits for them, and re-layouts: 6.63 us -> 0.11 us  [body(): term_slot.reshape(-1)]
  transfers between devices with their start and end apart: 4 -> 2, of which waited for: 2 -> 2; matrix products, arithmetic and copies ran while one was open for 1% -> 1% of each run, Pallas kernels for 0% -> 0%
where the time goes in v1:
time: 72 us; the launch traced here: 71.7 us
  blocking collectives  40.7 us (57%)
  starting transfers between devices  19.9 us (28%)
  Pallas kernels  4.47 us (6%)
  waiting for transfers between devices  3.37 us (5%)
  local copies, waits for them, and re-layouts  1.75 us (2%)
  other arithmetic  1.39 us (2%)
    all_gather x1, blocking collectives, body(): return lax.all_gather(owned, 'grp', axis=0, tiled=True).astype(jnp.float32)  20.8 us
    all_to_all x1, blocking collectives, body(): received = lax.all_to_all(blocks, 'dom', 0, 0, tiled=True)  19.9 us
    ppermute x1, starting transfers between devices, body(): from_far = lax.ppermute(to_far, ('grp', 'dom'), far)  18 us
    pallas_call x1, Pallas kernels, send_blocks(): pl.pallas_call(terms_kernel, out_shape=jax.ShapeDtypeStruct((count, 8 * B...  2.62 us
    ppermute x1, waiting for transfers between devices, body(): from_near = lax.ppermute(to_near, ('grp', 'dom'), near)  2.53 us
    ppermute x1, starting transfers between devices, body(): from_near = lax.ppermute(to_near, ('grp', 'dom'), near)  1.92 us
    pallas_call x1, Pallas kernels, pick(): pl.pallas_call(pick_kernel, out_shape=(shape, shape), in_specs=[pl.BlockS...  1.67 us
  transfers between devices with their start and end apart: 2, of which 2 were waited for; matrix products, arithmetic and copies ran while one was open for 1% of the time, Pallas kernels for 0%

profile of v1, /device:TPU:1, one launch (start us, length us, event | category | flops | bytes accessed | tf_op | source)
XLA Modules:
  0.0 71.7 jit_solution(15804946304682540739)
XLA Ops:
  0.0 0.0 copy-start.4
  0.0 0.0 copy-start.3
  0.0 1.7 %shard_map.64 = (bf16[4,128,128]{2,1,0:T(8,128)(2,1)}, bf16[4,128,128]{2,1,0:T(8,128)(2,1)}) custom-call(s32[1,8]{1,0:T(1,128)} %send_ref.1, bf16[4,128,128]{2,1,0:T(8,128)(2,1)} %p_ref.3), custom_call_target="tpu_custom_call" | custom-call | tf_op jit(solution)/shard_map/pallas_call | solution.py:38
  1.7 0.0 copy-start.1
  1.7 18.0 %collective-permute-start = (bf16[4,128,128]{2,1,0:T(8,128)(2,1)}, bf16[4,128,128]{2,1,0:T(8,128)(2,1)S(1)}, u32[]{:S(2)}, u32[]{:S(2)}) collective-permute-start(bf16[4,128,128]{2,1,0:T(8,128)(2,1)} %get-tuple-element.7), channel_id=1, source_target_pairs={{1,2},{2,1},{3,4},{4,3},{5,6},{6,5},{7,8},{8,7},{9,10},{10,9},{11,... | collective-permute-start | bytes 393224 | tf_op jit(solution)/shard_map/ppermute | solution.py:152
  19.7 1.9 %collective-permute-start.1 = (bf16[4,128,128]{2,1,0:T(8,128)(2,1)}, bf16[4,128,128]{2,1,0:T(8,128)(2,1)S(1)}, u32[]{:S(2)}, u32[]{:S(2)}) collective-permute-start(bf16[4,128,128]{2,1,0:T(8,128)(2,1)} %get-tuple-element.8), channel_id=1, source_target_pairs={{0,1},{1,0},{2,3},{3,2},{4,5},{5,4},{6,7},{7,6},{8,9},{9,8},{10,11... | collective-permute-start | bytes 393224 | tf_op jit(solution)/shard_map/ppermute | solution.py:153
  21.6 0.0 copy-done.4
  21.6 0.2 convert_reduce_fusion
  21.8 0.1 select_reduce_fusion
  21.9 0.0 copy-done.3
  22.0 0.2 copy.8
  22.1 0.1 reshape.12.slots_ref
  22.2 0.0 copy-start.2
  22.2 0.8 %collective-permute-done.far_ref = bf16[4,128,128]{2,1,0:T(8,128)(2,1)S(1)} collective-permute-done((bf16[4,128,128]{2,1,0:T(8,128)(2,1)}, bf16[4,128,128]{2,1,0:T(8,128)(2,1)S(1)}, u32[]{:S(2)}, u32[]{:S(2)}) %collective-permute-start) | collective-permute-done | bytes 131104 | tf_op jit(solution)/shard_map/ppermute | solution.py:152
  23.1 2.5 %collective-permute-done.1.near_ref = bf16[4,128,128]{2,1,0:T(8,128)(2,1)S(1)} collective-permute-done((bf16[4,128,128]{2,1,0:T(8,128)(2,1)}, bf16[4,128,128]{2,1,0:T(8,128)(2,1)S(1)}, u32[]{:S(2)}, u32[]{:S(2)}) %collective-permute-start.1) | collective-permute-done | bytes 131104 | tf_op jit(solution)/shard_map/ppermute | solution.py:153
  25.6 0.1 broadcast_in_dim.16.meta_ref
  25.7 0.0 copy-done.1
  25.7 0.0 copy-done.2
  25.7 0.0 copy-start
  25.7 1.2 %copy-done = bf16[4,8,128,128]{3,2,1,0:T(8,128)(2,1)S(1)} copy-done((bf16[4,8,128,128]{3,2,1,0:T(8,128)(2,1)S(1)}, bf16[4,8,128,128]{3,2,1,0:T(8,128)(2,1)}, u32[]{:S(2)}) %copy-start) | copy-done | bytes 1048600
  26.9 2.6 %shard_map.65 = bf16[96,1152]{1,0:T(8,128)(2,1)S(1)} custom-call(s32[4,8]{1,0:T(4,128)S(1)} %copy-done.2, s32[512]{0:T(512)S(1)} %reshape.12.slots_ref, s32[64]{0:T(128)S(1)} %multiply_add_fusion.pos_ref, bf16[96,128]{1,0:T(8,128)(2,1)S(1)} %broadcast_in_dim.16.meta_ref, bf16[4,8,128,128]{3,2,1,0:T(8,128)(2,1)S(1)} %copy-done, ...), custom_call_target="tpu_custom_call" | custom-call | flops 300000000 | bytes 2000000 | tf_op jit(solution)/shard_map/pallas_call | solution.py:113
  29.6 0.1 all_to_all.7
  29.7 19.9 %all_to_all.11 = bf16[48,2,1152]{2,1,0:T(2,128)(2,1)S(1)} all-to-all(bf16[48,2,1152]{2,1,0:T(2,128)(2,1)S(1)} %all_to_all.7), channel_id=1, replica_groups=mesh['grp'=16,'dom'=48] {'dom'}, dimensions={0} | all-to-all | bytes 442368 | tf_op jit(solution)/shard_map/all_to_all | solution.py:166
  49.6 0.1 all_to_all.9.in_ref
  49.7 0.2 shard_map.66
  49.9 20.8 %all_gather.3 = bf16[256,1024]{1,0:T(8,128)(2,1)S(1)} all-gather(bf16[16,1024]{1,0:T(8,128)(2,1)S(1)} %shard_map.66), channel_id=1, replica_groups=mesh['grp'=16,'dom'=48] {'grp'}, dimensions={0}, use_global_device_ids=true | all-gather | bytes 557056 | tf_op jit(solution)/shard_map/all_gather | solution.py:168
  70.6 1.1 %convert_element_type.15 = f32[256,1024]{1,0:T(8,128)} convert(bf16[256,1024]{1,0:T(8,128)(2,1)S(1)} %all_gather.3) | non-fusion elementwise | flops 262144 | bytes 1572864 | tf_op jit(solution)/shard_map/convert_element_type | solution.py:168
  (3 shorter events, 0.0 us)
Async XLA Ops:
  0.0 21.6 %copy-start.4 = (s32[64]{0:T(128)S(1)}, s32[64]{0:T(128)}, u32[]{:S(2)}) copy-start(s32[64]{0:T(128)} %param.11) | copy-start | bytes 772
  0.0 21.9 %copy-start.3 = (s32[4,4,8,4]{2,3,1,0:T(4,128)S(1)}, s32[4,4,8,4]{2,3,1,0:T(4,128)}, u32[]{:S(2)}) copy-start(s32[4,4,8,4]{2,3,1,0:T(4,128)} %param.10) | copy-start | bytes 6148
  1.7 24.0 %copy-start.1 = (bf16[4,128,128]{2,1,0:T(8,128)(2,1)S(1)}, bf16[4,128,128]{2,1,0:T(8,128)(2,1)}, u32[]{:S(2)}) copy-start(bf16[4,128,128]{2,1,0:T(8,128)(2,1)} %p_ref.3) | copy-start | bytes 393220
  1.7 21.4 %collective-permute-start = (bf16[4,128,128]{2,1,0:T(8,128)(2,1)}, bf16[4,128,128]{2,1,0:T(8,128)(2,1)S(1)}, u32[]{:S(2)}, u32[]{:S(2)}) collective-permute-start(bf16[4,128,128]{2,1,0:T(8,128)(2,1)} %get-tuple-element.7), channel_id=1, source_target_pairs={{1,2},{2,1},{3,4},{4,3},{5,6},{6,5},{7,8},{8,7},{9,10},{10,9},{11,... | collective-permute-start | bytes 393224 | tf_op jit(solution)/shard_map/ppermute | solution.py:152
  19.7 5.9 %collective-permute-start.1 = (bf16[4,128,128]{2,1,0:T(8,128)(2,1)}, bf16[4,128,128]{2,1,0:T(8,128)(2,1)S(1)}, u32[]{:S(2)}, u32[]{:S(2)}) collective-permute-start(bf16[4,128,128]{2,1,0:T(8,128)(2,1)} %get-tuple-element.8), channel_id=1, source_target_pairs={{0,1},{1,0},{2,3},{3,2},{4,5},{5,4},{6,7},{7,6},{8,9},{9,8},{10,11... | collective-permute-start | bytes 393224 | tf_op jit(solution)/shard_map/ppermute | solution.py:153
  22.2 3.5 %copy-start.2 = (s32[4,8]{1,0:T(4,128)S(1)}, s32[4,8]{1,0:T(4,128)}, u32[]{:S(2)}) copy-start(s32[4,8]{1,0:T(4,128)} %cols_ref.1) | copy-start | bytes 388
  25.7 1.2 %copy-start = (bf16[4,8,128,128]{3,2,1,0:T(8,128)(2,1)S(1)}, bf16[4,8,128,128]{3,2,1,0:T(8,128)(2,1)}, u32[]{:S(2)}) copy-start(bf16[4,8,128,128]{3,2,1,0:T(8,128)(2,1)} %a_ref.1) | copy-start | bytes 3145732

commit v2 on v1

--- a/solution.py
+++ b/solution.py
@@ -65,6 +65,27 @@
     return v0, v1, v2, v3
 
 
+def turn_kernel(a_ref, p_ref, turned_ref):
+    row = lax.broadcasted_iota(jnp.int32, (B, B), 0)
+    column = lax.broadcasted_iota(jnp.int32, (B, B), 1)
+    source = (row // 32) * 32 + 4 * (row % 8) + (row % 32) // 8
+    turn = (column == source).astype(jnp.bfloat16)
+    for n in range(NB):
+        turned_ref[n] = lax.dot_general(turn, p_ref[n], (((1,), (1,)), ((), ())), preferred_element_type=jnp.float32).astype(jnp.bfloat16)
+
+
+def turn_blocks(a_tiles, p_tiles):
+    vmem = pl.BlockSpec(memory_space=VMEM)
+    return pl.pallas_call(
+        turn_kernel,
+        out_shape=jax.ShapeDtypeStruct(p_tiles.shape, p_tiles.dtype),
+        in_specs=[vmem, vmem],
+        out_specs=vmem,
+        compiler_params=pltpu.CompilerParams(vmem_limit_bytes=MEDIUM),
+        cost_estimate=pl.CostEstimate(flops=20_000_000, bytes_accessed=1_400_000, transcendentals=0),
+    )(a_tiles, p_tiles)
+
+
 def add_terms(accs, places, terms):
     rows = [pl.ds(pl.multiple_of(place * 8, 8), 8) for place in places]
     sums = [acc[at, :] + term for acc, at, term in zip(accs, rows, terms)]
@@ -72,7 +93,7 @@
         acc[at, :] = value
 
 
-def terms_kernel(cols_ref, slots_ref, pos_ref, meta_ref, a_ref, p_ref, far_ref, near_ref, out_ref, table, product, *accs):
+def terms_kernel(cols_ref, slots_ref, pos_ref, meta_ref, a_ref, p_ref, turned_ref, far_ref, near_ref, out_ref, table, product, *accs):
     table[0:4] = p_ref[...]
     odd = is_odd()
     table[pl.ds(2 * NB - NB * odd, NB)] = near_ref[...]
@@ -80,12 +101,8 @@
     table[3 * NB] = jnp.zeros((B, B), jnp.bfloat16)
     for acc in accs:
         acc[...] = jnp.zeros_like(acc)
-    row = lax.broadcasted_iota(jnp.int32, (B, B), 0)
-    column = lax.broadcasted_iota(jnp.int32, (B, B), 1)
-    source = (row // 32) * 32 + 4 * (row % 8) + (row % 32) // 8
-    turn = (column == source).astype(jnp.bfloat16)
     for n in range(NB):
-        turned = lax.dot_general(turn, p_ref[n], (((1,), (1,)), ((), ())), preferred_element_type=jnp.float32).astype(jnp.bfloat16)
+        turned = turned_ref[n]
         for a in range(KA):
             product[n, :, a * B : (a + 1) * B] = jnp.dot(
                 a_ref[n, a], table[cols_ref[n, a]], preferred_element_type=jnp.float32
@@ -106,14 +123,14 @@
     out_ref[:, 8 * B :] = meta_ref[...]
 
 
-def send_blocks(a_cols, slots, pos, meta, a_tiles, p_tiles, far, near):
+def send_blocks(a_cols, slots, pos, meta, a_tiles, p_tiles, turned, far, near):
     count = meta.shape[0]
     vmem = pl.BlockSpec(memory_space=VMEM)
     smem = pl.BlockSpec(memory_space=SMEM)
     return pl.pallas_call(
         terms_kernel,
         out_shape=jax.ShapeDtypeStruct((count, 8 * B + META), jnp.bfloat16),
-        in_specs=[smem, smem, smem, vmem, vmem, vmem, vmem, vmem],
+        in_specs=[smem, smem, smem, vmem, vmem, vmem, vmem, vmem, vmem],
         out_specs=vmem,
         scratch_shapes=[
             VMEM((3 * NB + 1, B, B), jnp.bfloat16),
@@ -122,7 +139,7 @@
         + [VMEM((count * 8, B), jnp.float32)] * KP,
         compiler_params=pltpu.CompilerParams(vmem_limit_bytes=MEDIUM),
         cost_estimate=pl.CostEstimate(flops=300_000_000, bytes_accessed=2_000_000, transcendentals=0),
-    )(a_cols, slots, pos, meta, a_tiles, p_tiles, far, near)
+    )(a_cols, slots, pos, meta, a_tiles, p_tiles, turned, far, near)
 
 
 def owner_kernel(in_ref, out_ref):
@@ -152,6 +169,7 @@
     from_far = lax.ppermute(to_far, ("grp", "dom"), far)
     from_near = lax.ppermute(to_near, ("grp", "dom"), near)
 
+    turned = turn_blocks(a_tiles, p_tiles)
     rows = dom_count * CAP
     owner = owner_slot // (grp_count * OS)
     within = owner_slot % OS
@@ -162,7 +180,7 @@
     meta = jnp.sum(jnp.where(here, within[None, :], 0), axis=1).astype(jnp.bfloat16)
     meta = jnp.broadcast_to(meta[:, None], (rows, META))
 
-    blocks = send_blocks(a_cols, term_slot.reshape(-1), pos, meta, a_tiles, p_tiles, from_far, from_near)
+    blocks = send_blocks(a_cols, term_slot.reshape(-1), pos, meta, a_tiles, p_tiles, turned, from_far, from_near)
     received = lax.all_to_all(blocks, "dom", 0, 0, tiled=True)
     owned = own_sum(received)
     return lax.all_gather(owned, "grp", axis=0, tiled=True).astype(jnp.float32)

time: 72 us -> 70.8 us (0.983)
  waiting for transfers between devices: 3.37 us -> 1.17 us
  local copies, waits for them, and re-layouts: 1.75 us -> 2.5 us
    ppermute x1, waiting for transfers between devices: 2.53 us -> 1.16 us  [body(): from_near = lax.ppermute(to_near, ('grp', 'dom'), near)]
    ppermute x1, waiting for transfers between devices: 0.84 us -> 0.01 us  [body(): from_far = lax.ppermute(to_far, ('grp', 'dom'), far)]
    unnamed x11 -> x9, local copies, waits for them, and re-layouts: 1.41 us -> 2.16 us
  transfers between devices with their start and end apart: 2 -> 2, of which waited for: 2 -> 1; matrix products, arithmetic and copies ran while one was open for 1% -> 2% of each run, Pallas kernels for 0% -> 0%
where the time goes in v2:
time: 70.8 us; the launch traced here: 70.5 us
  blocking collectives  40.7 us (57%)
  starting transfers between devices  19.9 us (28%)
  Pallas kernels  4.68 us (7%)
  local copies, waits for them, and re-layouts  2.5 us (4%)
  other arithmetic  1.39 us (2%)
  waiting for transfers between devices  1.17 us (2%)
    all_gather x1, blocking collectives, body(): return lax.all_gather(owned, 'grp', axis=0, tiled=True).astype(jnp.float32)  20.8 us
    all_to_all x1, blocking collectives, body(): received = lax.all_to_all(blocks, 'dom', 0, 0, tiled=True)  20 us
    ppermute x1, starting transfers between devices, body(): from_far = lax.ppermute(to_far, ('grp', 'dom'), far)  18 us
    pallas_call x1, Pallas kernels, send_blocks(): pl.pallas_call(terms_kernel, out_shape=jax.ShapeDtypeStruct((count, 8 * B...  2.58 us
    unnamed x9, local copies, waits for them, and re-layouts  2.16 us
    ppermute x1, starting transfers between devices, body(): from_near = lax.ppermute(to_near, ('grp', 'dom'), near)  1.92 us
    pallas_call x1, Pallas kernels, pick(): pl.pallas_call(pick_kernel, out_shape=(shape, shape), in_specs=[pl.BlockS...  1.72 us
  transfers between devices with their start and end apart: 2, of which 1 were waited for; matrix products, arithmetic and copies ran while one was open for 2% of the time, Pallas kernels for 0%

profile of v2, /device:TPU:1, one launch (start us, length us, event | category | flops | bytes accessed | tf_op | source)
XLA Modules:
  0.0 70.5 jit_solution(8505854156704338746)
XLA Ops:
  0.0 0.0 copy-start.1
  0.0 1.7 %shard_map.65 = (bf16[4,128,128]{2,1,0:T(8,128)(2,1)}, bf16[4,128,128]{2,1,0:T(8,128)(2,1)}) custom-call(s32[1,8]{1,0:T(1,128)} %send_ref.1, bf16[4,128,128]{2,1,0:T(8,128)(2,1)} %p_ref.5), custom_call_target="tpu_custom_call" | custom-call | tf_op jit(solution)/shard_map/pallas_call | solution.py:38
  1.7 0.0 copy-start.3
  1.7 18.0 %collective-permute-start = (bf16[4,128,128]{2,1,0:T(8,128)(2,1)}, bf16[4,128,128]{2,1,0:T(8,128)(2,1)S(1)}, u32[]{:S(2)}, u32[]{:S(2)}) collective-permute-start(bf16[4,128,128]{2,1,0:T(8,128)(2,1)} %get-tuple-element.7), channel_id=1, source_target_pairs={{1,2},{2,1},{3,4},{4,3},{5,6},{6,5},{7,8},{8,7},{9,10},{10,9},{11,... | collective-permute-start | bytes 393224 | tf_op jit(solution)/shard_map/ppermute | solution.py:169
  19.7 1.9 %collective-permute-start.1 = (bf16[4,128,128]{2,1,0:T(8,128)(2,1)}, bf16[4,128,128]{2,1,0:T(8,128)(2,1)S(1)}, u32[]{:S(2)}, u32[]{:S(2)}) collective-permute-start(bf16[4,128,128]{2,1,0:T(8,128)(2,1)} %get-tuple-element.8), channel_id=1, source_target_pairs={{0,1},{1,0},{2,3},{3,2},{4,5},{5,4},{6,7},{7,6},{8,9},{9,8},{10,11... | collective-permute-start | bytes 393224 | tf_op jit(solution)/shard_map/ppermute | solution.py:170
  21.7 0.0 copy-done.3
  21.7 0.2 convert_reduce_fusion
  21.9 0.1 select_reduce_fusion
  22.0 0.9 %copy.8 = s32[4,4,8,4]{3,2,1,0:T(8,128)S(1)} copy(s32[4,4,8,4]{2,3,1,0:T(4,128)} %param.10) | data formatting | bytes 4096 | tf_op args[4]
  22.9 0.1 reshape.12.slots_ref
  23.0 0.0 copy-done.1
  23.0 0.0 copy-start
  23.0 1.2 %copy-done = bf16[4,8,128,128]{3,2,1,0:T(8,128)(2,1)S(1)} copy-done((bf16[4,8,128,128]{3,2,1,0:T(8,128)(2,1)S(1)}, bf16[4,8,128,128]{3,2,1,0:T(8,128)(2,1)}, u32[]{:S(2)}) %copy-start) | copy-done | bytes 1048600
  24.3 0.2 shard_map.64.turned_ref
  24.5 0.0 copy-start.2
  24.5 0.0 collective-permute-done.far_ref
  24.5 1.2 %collective-permute-done.1.near_ref = bf16[4,128,128]{2,1,0:T(8,128)(2,1)S(1)} collective-permute-done((bf16[4,128,128]{2,1,0:T(8,128)(2,1)}, bf16[4,128,128]{2,1,0:T(8,128)(2,1)S(1)}, u32[]{:S(2)}, u32[]{:S(2)}) %collective-permute-start.1) | collective-permute-done | bytes 131104 | tf_op jit(solution)/shard_map/ppermute | solution.py:170
  25.7 0.1 broadcast_in_dim.16.meta_ref
  25.7 0.0 copy-done.2
  25.7 2.6 %shard_map.66 = bf16[96,1152]{1,0:T(8,128)(2,1)S(1)} custom-call(s32[4,8]{1,0:T(4,128)S(1)} %copy-done.2, s32[512]{0:T(512)S(1)} %reshape.12.slots_ref, s32[64]{0:T(128)S(1)} %multiply_add_fusion.pos_ref, bf16[96,128]{1,0:T(8,128)(2,1)S(1)} %broadcast_in_dim.16.meta_ref, bf16[4,8,128,128]{3,2,1,0:T(8,128)(2,1)S(1)} %copy-done, ...), custom_call_target="tpu_custom_call" | custom-call | flops 300000000 | bytes 2000000 | tf_op jit(solution)/shard_map/pallas_call | solution.py:130
  28.3 0.1 all_to_all.7
  28.4 20.0 %all_to_all.11 = bf16[48,2,1152]{2,1,0:T(2,128)(2,1)S(1)} all-to-all(bf16[48,2,1152]{2,1,0:T(2,128)(2,1)S(1)} %all_to_all.7), channel_id=1, replica_groups=mesh['grp'=16,'dom'=48] {'dom'}, dimensions={0} | all-to-all | bytes 442368 | tf_op jit(solution)/shard_map/all_to_all | solution.py:184
  48.4 0.1 all_to_all.9.in_ref
  48.5 0.2 shard_map.67
  48.6 20.8 %all_gather.3 = bf16[256,1024]{1,0:T(8,128)(2,1)S(1)} all-gather(bf16[16,1024]{1,0:T(8,128)(2,1)S(1)} %shard_map.67), channel_id=1, replica_groups=mesh['grp'=16,'dom'=48] {'grp'}, dimensions={0}, use_global_device_ids=true | all-gather | bytes 557056 | tf_op jit(solution)/shard_map/all_gather | solution.py:186
  69.4 1.1 %convert_element_type.15 = f32[256,1024]{1,0:T(8,128)} convert(bf16[256,1024]{1,0:T(8,128)(2,1)S(1)} %all_gather.3) | non-fusion elementwise | flops 262144 | bytes 1572864 | tf_op jit(solution)/shard_map/convert_element_type | solution.py:186
  (3 shorter events, 0.0 us)
Async XLA Ops:
  0.0 23.0 %copy-start.1 = (bf16[4,128,128]{2,1,0:T(8,128)(2,1)S(1)}, bf16[4,128,128]{2,1,0:T(8,128)(2,1)}, u32[]{:S(2)}) copy-start(bf16[4,128,128]{2,1,0:T(8,128)(2,1)} %p_ref.5) | copy-start | bytes 393220
  1.7 19.9 %copy-start.3 = (s32[64]{0:T(128)S(1)}, s32[64]{0:T(128)}, u32[]{:S(2)}) copy-start(s32[64]{0:T(128)} %param.11) | copy-start | bytes 772
  1.7 22.8 %collective-permute-start = (bf16[4,128,128]{2,1,0:T(8,128)(2,1)}, bf16[4,128,128]{2,1,0:T(8,128)(2,1)S(1)}, u32[]{:S(2)}, u32[]{:S(2)}) collective-permute-start(bf16[4,128,128]{2,1,0:T(8,128)(2,1)} %get-tuple-element.7), channel_id=1, source_target_pairs={{1,2},{2,1},{3,4},{4,3},{5,6},{6,5},{7,8},{8,7},{9,10},{10,9},{11,... | collective-permute-start | bytes 393224 | tf_op jit(solution)/shard_map/ppermute | solution.py:169
  19.7 5.9 %collective-permute-start.1 = (bf16[4,128,128]{2,1,0:T(8,128)(2,1)}, bf16[4,128,128]{2,1,0:T(8,128)(2,1)S(1)}, u32[]{:S(2)}, u32[]{:S(2)}) collective-permute-start(bf16[4,128,128]{2,1,0:T(8,128)(2,1)} %get-tuple-element.8), channel_id=1, source_target_pairs={{0,1},{1,0},{2,3},{3,2},{4,5},{5,4},{6,7},{7,6},{8,9},{9,8},{10,11... | collective-permute-start | bytes 393224 | tf_op jit(solution)/shard_map/ppermute | solution.py:170
  23.0 1.2 %copy-start = (bf16[4,8,128,128]{3,2,1,0:T(8,128)(2,1)S(1)}, bf16[4,8,128,128]{3,2,1,0:T(8,128)(2,1)}, u32[]{:S(2)}) copy-start(bf16[4,8,128,128]{3,2,1,0:T(8,128)(2,1)} %a_ref.3) | copy-start | bytes 3145732
  24.5 1.3 %copy-start.2 = (s32[4,8]{1,0:T(4,128)S(1)}, s32[4,8]{1,0:T(4,128)}, u32[]{:S(2)}) copy-start(s32[4,8]{1,0:T(4,128)} %cols_ref.1) | copy-start | bytes 388

commit v3 on v2

--- a/solution.py
+++ b/solution.py
@@ -16,7 +16,6 @@
 META = 128
 SMALL = 4 * 1024 * 1024
 MEDIUM = 16 * 1024 * 1024
-PICK_GRANT = 60 * 1024 * 1024
 VMEM = pltpu.VMEM
 SMEM = pltpu.SMEM
 
@@ -25,23 +24,11 @@
     return lax.rem(lax.axis_index("dom"), 2)
 
 
-def pick_kernel(send_ref, p_ref, far_ref, near_ref):
-    to_far = NB * is_odd()
-    to_near = NB - to_far
-    for k in range(NB):
-        near_ref[k] = p_ref[send_ref[0, to_near + k]]
-        far_ref[k] = p_ref[send_ref[0, to_far + k]]
-
-
-def pick(send_list, p_tiles):
-    shape = jax.ShapeDtypeStruct(p_tiles.shape, p_tiles.dtype)
-    return pl.pallas_call(
-        pick_kernel,
-        out_shape=(shape, shape),
-        in_specs=[pl.BlockSpec(memory_space=SMEM), pl.BlockSpec(memory_space=VMEM)],
-        out_specs=(pl.BlockSpec(memory_space=VMEM),) * 2,
-        compiler_params=pltpu.CompilerParams(vmem_limit_bytes=PICK_GRANT),
-    )(send_list, p_tiles)
+def chosen(entries, p_tiles):
+    picked = jnp.broadcast_to(p_tiles[NB - 1], p_tiles.shape)
+    for k in range(NB - 1):
+        picked = jnp.where(entries[:, None, None] == k, p_tiles[k], picked)
+    return picked
 
 
 def lane_turn(v):
@@ -93,7 +80,7 @@
         acc[at, :] = value
 
 
-def terms_kernel(cols_ref, slots_ref, pos_ref, meta_ref, a_ref, p_ref, turned_ref, far_ref, near_ref, out_ref, table, product, *accs):
+def terms_kernel(cols_ref, slots_ref, pos_ref, meta_ref, a_ref, p_ref, turned_ref, near_ref, far_ref, out_ref, table, product, *accs):
     table[0:4] = p_ref[...]
     odd = is_odd()
     table[pl.ds(2 * NB - NB * odd, NB)] = near_ref[...]
@@ -116,14 +103,14 @@
                     first = ((n * KP + q) * KA + a + half) * KP
                     add_terms(accs, [pos_ref[slots_ref[first + p]] for p in range(KP)], lane_turn(v))
     count = out_ref.shape[0]
+    first = accs[0]
+    first[...] = (accs[0][...] + accs[1][...]) + (accs[2][...] + accs[3][...])
     for i in range(8):
-        parts = [acc[pl.ds(i, count, stride=8), :] for acc in accs]
-        total = (parts[0] + parts[1]) + (parts[2] + parts[3])
-        out_ref[:, i * B : (i + 1) * B] = total.astype(jnp.bfloat16)
+        out_ref[:, i * B : (i + 1) * B] = first[pl.ds(i, count, stride=8), :].astype(jnp.bfloat16)
     out_ref[:, 8 * B :] = meta_ref[...]
 
 
-def send_blocks(a_cols, slots, pos, meta, a_tiles, p_tiles, turned, far, near):
+def send_blocks(a_cols, slots, pos, meta, a_tiles, p_tiles, turned, near, far):
     count = meta.shape[0]
     vmem = pl.BlockSpec(memory_space=VMEM)
     smem = pl.BlockSpec(memory_space=SMEM)
@@ -139,7 +126,7 @@
         + [VMEM((count * 8, B), jnp.float32)] * KP,
         compiler_params=pltpu.CompilerParams(vmem_limit_bytes=MEDIUM),
         cost_estimate=pl.CostEstimate(flops=300_000_000, bytes_accessed=2_000_000, transcendentals=0),
-    )(a_cols, slots, pos, meta, a_tiles, p_tiles, turned, far, near)
+    )(a_cols, slots, pos, meta, a_tiles, p_tiles, turned, near, far)
 
 
 def owner_kernel(in_ref, out_ref):
@@ -163,7 +150,10 @@
     dom_count = lax.axis_size("dom")
     grp_count = lax.axis_size("grp")
     devices = dom_count * grp_count
-    to_far, to_near = pick(send_list, p_tiles)
+    odd = is_odd() == 1
+    to_lower, to_higher = send_list[0, :NB], send_list[0, NB:]
+    to_far = chosen(jnp.where(odd, to_higher, to_lower), p_tiles)
+    to_near = chosen(jnp.where(odd, to_lower, to_higher), p_tiles)
     near = [(i, i ^ 1) for i in range(devices)]
     far = [(i, ((i + 1) ^ 1) - 1) for i in range(1, devices - 1)]
     from_far = lax.ppermute(to_far, ("grp", "dom"), far)
@@ -180,7 +170,7 @@
     meta = jnp.sum(jnp.where(here, within[None, :], 0), axis=1).astype(jnp.bfloat16)
     meta = jnp.broadcast_to(meta[:, None], (rows, META))
 
-    blocks = send_blocks(a_cols, term_slot.reshape(-1), pos, meta, a_tiles, p_tiles, turned, from_far, from_near)
+    blocks = send_blocks(a_cols, term_slot.reshape(-1), pos, meta, a_tiles, p_tiles, turned, from_near, from_far)
     received = lax.all_to_all(blocks, "dom", 0, 0, tiled=True)
     owned = own_sum(received)
     return lax.all_gather(owned, "grp", axis=0, tiled=True).astype(jnp.float32)

time: 70.8 us -> 69.9 us (0.987)
  Pallas kernels: 4.68 us -> 2.85 us
    pallas_call x1 -> x0, Pallas kernels: 1.72 us -> none  [pick(): pl.pallas_call(pick_kernel, out_shape=(shape, shape), in_specs=[pl.BlockS...]
    squeeze x0 -> x1, local copies, waits for them, and re-layouts: none -> 0.83 us  [chosen(): picked = jnp.where(entries[:, None, None] == k, p_tiles[k], picked)]
    unnamed x9 -> x13, local copies, waits for them, and re-layouts: 2.16 us -> 1.42 us
  transfers between devices with their start and end apart: 2 -> 2, of which waited for: 1 -> 1; matrix products, arithmetic and copies ran while one was open for 2% -> 1% of each run, Pallas kernels for 0% -> 0%
where the time goes in v3:
time: 69.9 us; the launch traced here: 69.6 us
  blocking collectives  40.7 us (58%)
  starting transfers between devices  19.9 us (28%)
  Pallas kernels  2.85 us (4%)
  local copies, waits for them, and re-layouts  2.6 us (4%)
  waiting for transfers between devices  1.7 us (2%)
  other arithmetic  1.59 us (2%)
    all_gather x1, blocking collectives, body(): return lax.all_gather(owned, 'grp', axis=0, tiled=True).astype(jnp.float32)  20.8 us
    all_to_all x1, blocking collectives, body(): received = lax.all_to_all(blocks, 'dom', 0, 0, tiled=True)  20 us
    ppermute x1, starting transfers between devices, body(): from_far = lax.ppermute(to_far, ('grp', 'dom'), far)  18 us
    pallas_call x1, Pallas kernels, send_blocks(): pl.pallas_call(terms_kernel, out_shape=jax.ShapeDtypeStruct((count, 8 * B...  2.46 us
    ppermute x1, starting transfers between devices, body(): from_near = lax.ppermute(to_near, ('grp', 'dom'), near)  1.92 us
    ppermute x1, waiting for transfers between devices, body(): from_near = lax.ppermute(to_near, ('grp', 'dom'), near)  1.69 us
    unnamed x13, local copies, waits for them, and re-layouts  1.42 us
  transfers between devices with their start and end apart: 2, of which 1 were waited for; matrix products, arithmetic and copies ran while one was open for 1% of the time, Pallas kernels for 0%

profile of v3, /device:TPU:1, one launch (start us, length us, event | category | flops | bytes accessed | tf_op | source)
XLA Modules:
  0.0 69.6 jit_solution(11431173713385185742)
XLA Ops:
  0.0 0.0 copy-start.4
  0.0 0.8 %slice_bitcast_fusion.3 = (bf16[128,128]{1,0:T(8,128)(2,1)S(1)}, bf16[128,128]{1,0:T(8,128)(2,1)S(1)}, bf16[128,128]{1,0:T(8,128)(2,1)S(1)}, bf16[128,128]{1,0:T(8,128)(2,1)S(1)}) fusion(bf16[4,128,128]{2,1,0:T(8,128)(2,1)} %p_ref.3), kind=kLoop, calls=%fused_computation.5 | loop fusion | bytes 262144 | tf_op jit(solution)/shard_map/squeeze | solution.py:30
  0.8 0.0 copy-done.4
  0.8 0.1 compare_bitcast_fusion.2
  0.9 0.0 copy-start.5
  0.9 0.0 copy-start.3
  1.0 0.1 select_select_fusion
  1.1 0.0 copy-start.1
  1.1 18.0 %collective-permute-start.1 = (bf16[4,128,128]{2,1,0:T(8,128)(2,1)S(1)}, bf16[4,128,128]{2,1,0:T(8,128)(2,1)S(1)}, u32[]{:S(2)}, u32[]{:S(2)}) collective-permute-start(bf16[4,128,128]{2,1,0:T(8,128)(2,1)S(1)} %get-tuple-element.9), channel_id=1, source_target_pairs={{1,2},{2,1},{3,4},{4,3},{5,6},{6,5},{7,8},{8,7},{9,10},{10,9},{11,... | collective-permute-start | bytes 393224 | tf_op jit(solution)/shard_map/ppermute | solution.py:159
  19.1 1.9 %collective-permute-start = (bf16[4,128,128]{2,1,0:T(8,128)(2,1)S(1)}, bf16[4,128,128]{2,1,0:T(8,128)(2,1)S(1)}, u32[]{:S(2)}, u32[]{:S(2)}) collective-permute-start(bf16[4,128,128]{2,1,0:T(8,128)(2,1)S(1)} %get-tuple-element.10), channel_id=1, source_target_pairs={{0,1},{1,0},{2,3},{3,2},{4,5},{5,4},{6,7},{7,6},{8,9},{9,8},{10,11... | collective-permute-start | bytes 393224 | tf_op jit(solution)/shard_map/ppermute | solution.py:160
  21.1 0.0 copy-done.5
  21.1 0.2 convert_reduce_fusion
  21.3 0.1 select_reduce_fusion
  21.4 0.0 copy-done.3
  21.4 0.2 copy.8
  21.6 0.1 reshape.82.slots_ref
  21.7 0.0 copy-done.1
  21.7 0.0 copy-start
  21.7 1.2 %copy-done = bf16[4,8,128,128]{3,2,1,0:T(8,128)(2,1)S(1)} copy-done((bf16[4,8,128,128]{3,2,1,0:T(8,128)(2,1)S(1)}, bf16[4,8,128,128]{3,2,1,0:T(8,128)(2,1)}, u32[]{:S(2)}) %copy-start) | copy-done | bytes 1048600
  22.9 0.2 shard_map.64.turned_ref
  23.1 0.0 copy-start.2
  23.1 0.0 collective-permute-done.1.far_ref
  23.1 1.7 %collective-permute-done.near_ref = bf16[4,128,128]{2,1,0:T(8,128)(2,1)S(1)} collective-permute-done((bf16[4,128,128]{2,1,0:T(8,128)(2,1)S(1)}, bf16[4,128,128]{2,1,0:T(8,128)(2,1)S(1)}, u32[]{:S(2)}, u32[]{:S(2)}) %collective-permute-start) | collective-permute-done | bytes 131104 | tf_op jit(solution)/shard_map/ppermute | solution.py:160
  24.8 0.1 broadcast_in_dim.83.meta_ref
  24.9 0.0 copy-done.2
  24.9 2.5 %shard_map.65 = bf16[96,1152]{1,0:T(8,128)(2,1)S(1)} custom-call(s32[4,8]{1,0:T(4,128)S(1)} %copy-done.2, s32[512]{0:T(512)S(1)} %reshape.82.slots_ref, s32[64]{0:T(128)S(1)} %multiply_add_fusion.pos_ref, bf16[96,128]{1,0:T(8,128)(2,1)S(1)} %broadcast_in_dim.83.meta_ref, bf16[4,8,128,128]{3,2,1,0:T(8,128)(2,1)S(1)} %copy-done, ...), custom_call_target="tpu_custom_call" | custom-call | flops 300000000 | bytes 2000000 | tf_op jit(solution)/shard_map/pallas_call | solution.py:117
  27.4 0.1 all_to_all.7
  27.5 20.0 %all_to_all.11 = bf16[48,2,1152]{2,1,0:T(2,128)(2,1)S(1)} all-to-all(bf16[48,2,1152]{2,1,0:T(2,128)(2,1)S(1)} %all_to_all.7), channel_id=1, replica_groups=mesh['grp'=16,'dom'=48] {'dom'}, dimensions={0} | all-to-all | bytes 442368 | tf_op jit(solution)/shard_map/all_to_all | solution.py:174
  47.4 0.1 all_to_all.9.in_ref
  47.5 0.2 shard_map.66
  47.7 20.8 %all_gather.3 = bf16[256,1024]{1,0:T(8,128)(2,1)S(1)} all-gather(bf16[16,1024]{1,0:T(8,128)(2,1)S(1)} %shard_map.66), channel_id=1, replica_groups=mesh['grp'=16,'dom'=48] {'grp'}, dimensions={0}, use_global_device_ids=true | all-gather | bytes 557056 | tf_op jit(solution)/shard_map/all_gather | solution.py:176
  68.5 1.1 %convert_element_type.15 = f32[256,1024]{1,0:T(8,128)} convert(bf16[256,1024]{1,0:T(8,128)(2,1)S(1)} %all_gather.3) | non-fusion elementwise | flops 262144 | bytes 1572864 | tf_op jit(solution)/shard_map/convert_element_type | solution.py:176
  (4 shorter events, 0.0 us)
Async XLA Ops:
  0.0 0.8 %copy-start.4 = (s32[1,8]{1,0:T(1,128)S(1)}, s32[1,8]{1,0:T(1,128)}, u32[]{:S(2)}) copy-start(s32[1,8]{1,0:T(1,128)} %param.9) | copy-start | bytes 100
  0.9 20.1 %copy-start.5 = (s32[64]{0:T(128)S(1)}, s32[64]{0:T(128)}, u32[]{:S(2)}) copy-start(s32[64]{0:T(128)} %param.11) | copy-start | bytes 772
  0.9 20.4 %copy-start.3 = (s32[4,4,8,4]{2,3,1,0:T(4,128)S(1)}, s32[4,4,8,4]{2,3,1,0:T(4,128)}, u32[]{:S(2)}) copy-start(s32[4,4,8,4]{2,3,1,0:T(4,128)} %param.10) | copy-start | bytes 6148
  1.1 20.6 %copy-start.1 = (bf16[4,128,128]{2,1,0:T(8,128)(2,1)S(1)}, bf16[4,128,128]{2,1,0:T(8,128)(2,1)}, u32[]{:S(2)}) copy-start(bf16[4,128,128]{2,1,0:T(8,128)(2,1)} %p_ref.3) | copy-start | bytes 393220
  1.1 22.0 %collective-permute-start.1 = (bf16[4,128,128]{2,1,0:T(8,128)(2,1)S(1)}, bf16[4,128,128]{2,1,0:T(8,128)(2,1)S(1)}, u32[]{:S(2)}, u32[]{:S(2)}) collective-permute-start(bf16[4,128,128]{2,1,0:T(8,128)(2,1)S(1)} %get-tuple-element.9), channel_id=1, source_target_pairs={{1,2},{2,1},{3,4},{4,3},{5,6},{6,5},{7,8},{8,7},{9,10},{10,9},{11,... | collective-permute-start | bytes 393224 | tf_op jit(solution)/shard_map/ppermute | solution.py:159
  19.1 5.7 %collective-permute-start = (bf16[4,128,128]{2,1,0:T(8,128)(2,1)S(1)}, bf16[4,128,128]{2,1,0:T(8,128)(2,1)S(1)}, u32[]{:S(2)}, u32[]{:S(2)}) collective-permute-start(bf16[4,128,128]{2,1,0:T(8,128)(2,1)S(1)} %get-tuple-element.10), channel_id=1, source_target_pairs={{0,1},{1,0},{2,3},{3,2},{4,5},{5,4},{6,7},{7,6},{8,9},{9,8},{10,11... | collective-permute-start | bytes 393224 | tf_op jit(solution)/shard_map/ppermute | solution.py:160
  21.7 1.2 %copy-start = (bf16[4,8,128,128]{3,2,1,0:T(8,128)(2,1)S(1)}, bf16[4,8,128,128]{3,2,1,0:T(8,128)(2,1)}, u32[]{:S(2)}) copy-start(bf16[4,8,128,128]{3,2,1,0:T(8,128)(2,1)} %a_ref.3) | copy-start | bytes 3145732
  23.1 1.8 %copy-start.2 = (s32[4,8]{1,0:T(4,128)S(1)}, s32[4,8]{1,0:T(4,128)}, u32[]{:S(2)}) copy-start(s32[4,8]{1,0:T(4,128)} %cols_ref.1) | copy-start | bytes 388

commit v4 on v3

--- a/solution.py
+++ b/solution.py
@@ -14,6 +14,7 @@
 OS = 16
 CAP = 2
 META = 128
+PARTS = 4
 SMALL = 4 * 1024 * 1024
 MEDIUM = 16 * 1024 * 1024
 VMEM = pltpu.VMEM
@@ -146,6 +147,29 @@
     )(received)
 
 
+def widen_kernel(in_ref, out_ref, wide, sems):
+    rows = in_ref.shape[0] // PARTS
+    copies = []
+    for i in range(PARTS):
+        at = pl.ds(i * rows, rows)
+        wide[at, :] = in_ref[at, :].astype(jnp.float32)
+        copies.append(pltpu.make_async_copy(wide.at[at], out_ref.at[at], sems.at[i]))
+        copies[-1].start()
+    for copy in copies:
+        copy.wait()
+
+
+def widen(gathered):
+    return pl.pallas_call(
+        widen_kernel,
+        out_shape=jax.ShapeDtypeStruct(gathered.shape, jnp.float32),
+        in_specs=[pl.BlockSpec(memory_space=VMEM)],
+        out_specs=pl.BlockSpec(memory_space=pltpu.HBM),
+        scratch_shapes=[VMEM(gathered.shape, jnp.float32), pltpu.SemaphoreType.DMA((PARTS,))],
+        compiler_params=pltpu.CompilerParams(vmem_limit_bytes=MEDIUM),
+    )(gathered)
+
+
 def body(a_tiles, a_cols, p_tiles, send_list, term_slot, owner_slot):
     dom_count = lax.axis_size("dom")
     grp_count = lax.axis_size("grp")
@@ -173,7 +197,7 @@
     blocks = send_blocks(a_cols, term_slot.reshape(-1), pos, meta, a_tiles, p_tiles, turned, from_near, from_far)
     received = lax.all_to_all(blocks, "dom", 0, 0, tiled=True)
     owned = own_sum(received)
-    return lax.all_gather(owned, "grp", axis=0, tiled=True).astype(jnp.float32)
+    return widen(lax.all_gather(owned, "grp", axis=0, tiled=True))
 
 
 def solution(mesh):

time: 69.9 us -> 69.8 us (level)
  other arithmetic: 1.59 us -> 0.51 us
  Pallas kernels: 2.85 us -> 3.86 us
    convert_element_type x1 -> x0, other arithmetic: 1.09 us -> none  [body(): return lax.all_gather(owned, 'grp', axis=0, tiled=True).astype(jnp.float32)]
    pallas_call x0 -> x1, Pallas kernels: none -> 1.01 us  [widen(): pl.pallas_call(widen_kernel, out_shape=jax.ShapeDtypeStruct(gathered.shap...]
where the time goes in v4:
time: 69.8 us; the launch traced here: 69.5 us
  blocking collectives  40.7 us (58%)
  starting transfers between devices  19.9 us (29%)
  Pallas kernels  3.86 us (6%)
  local copies, waits for them, and re-layouts  2.6 us (4%)
  waiting for transfers between devices  1.7 us (2%)
    all_gather x1, blocking collectives, body(): return widen(lax.all_gather(owned, 'grp', axis=0, tiled=True))  20.8 us
    all_to_all x1, blocking collectives, body(): received = lax.all_to_all(blocks, 'dom', 0, 0, tiled=True)  19.9 us
    ppermute x1, starting transfers between devices, body(): from_far = lax.ppermute(to_far, ('grp', 'dom'), far)  18 us
    pallas_call x1, Pallas kernels, send_blocks(): pl.pallas_call(terms_kernel, out_shape=jax.ShapeDtypeStruct((count, 8 * B...  2.46 us
    ppermute x1, starting transfers between devices, body(): from_near = lax.ppermute(to_near, ('grp', 'dom'), near)  1.92 us
    ppermute x1, waiting for transfers between devices, body(): from_near = lax.ppermute(to_near, ('grp', 'dom'), near)  1.69 us
    unnamed x13, local copies, waits for them, and re-layouts  1.42 us
  transfers between devices with their start and end apart: 2, of which 1 were waited for; matrix products, arithmetic and copies ran while one was open for 1% of the time, Pallas kernels for 0%

profile of v4, /device:TPU:1, one launch (start us, length us, event | category | flops | bytes accessed | tf_op | source)
XLA Modules:
  0.0 69.5 jit_solution(6762340191520785632)
XLA Ops:
  0.0 0.0 copy-start.4
  0.0 0.8 %slice_bitcast_fusion.3 = (bf16[128,128]{1,0:T(8,128)(2,1)S(1)}, bf16[128,128]{1,0:T(8,128)(2,1)S(1)}, bf16[128,128]{1,0:T(8,128)(2,1)S(1)}, bf16[128,128]{1,0:T(8,128)(2,1)S(1)}) fusion(bf16[4,128,128]{2,1,0:T(8,128)(2,1)} %p_ref.3), kind=kLoop, calls=%fused_computation.5 | loop fusion | bytes 262144 | tf_op jit(solution)/shard_map/squeeze | solution.py:31
  0.8 0.0 copy-done.4
  0.8 0.1 compare_bitcast_fusion.2
  0.9 0.0 copy-start.5
  0.9 0.0 copy-start.3
  1.0 0.1 select_select_fusion
  1.1 0.0 copy-start.1
  1.1 18.0 %collective-permute-start.1 = (bf16[4,128,128]{2,1,0:T(8,128)(2,1)S(1)}, bf16[4,128,128]{2,1,0:T(8,128)(2,1)S(1)}, u32[]{:S(2)}, u32[]{:S(2)}) collective-permute-start(bf16[4,128,128]{2,1,0:T(8,128)(2,1)S(1)} %get-tuple-element.9), channel_id=1, source_target_pairs={{1,2},{2,1},{3,4},{4,3},{5,6},{6,5},{7,8},{8,7},{9,10},{10,9},{11,... | collective-permute-start | bytes 393224 | tf_op jit(solution)/shard_map/ppermute | solution.py:183
  19.1 1.9 %collective-permute-start = (bf16[4,128,128]{2,1,0:T(8,128)(2,1)S(1)}, bf16[4,128,128]{2,1,0:T(8,128)(2,1)S(1)}, u32[]{:S(2)}, u32[]{:S(2)}) collective-permute-start(bf16[4,128,128]{2,1,0:T(8,128)(2,1)S(1)} %get-tuple-element.10), channel_id=1, source_target_pairs={{0,1},{1,0},{2,3},{3,2},{4,5},{5,4},{6,7},{7,6},{8,9},{9,8},{10,11... | collective-permute-start | bytes 393224 | tf_op jit(solution)/shard_map/ppermute | solution.py:184
  21.1 0.0 copy-done.5
  21.1 0.2 convert_reduce_fusion
  21.3 0.1 select_reduce_fusion
  21.4 0.0 copy-done.3
  21.4 0.2 copy.8
  21.6 0.1 reshape.82.slots_ref
  21.7 0.0 copy-done.1
  21.7 0.0 copy-start
  21.7 1.2 %copy-done = bf16[4,8,128,128]{3,2,1,0:T(8,128)(2,1)S(1)} copy-done((bf16[4,8,128,128]{3,2,1,0:T(8,128)(2,1)S(1)}, bf16[4,8,128,128]{3,2,1,0:T(8,128)(2,1)}, u32[]{:S(2)}) %copy-start) | copy-done | bytes 1048600
  22.9 0.2 shard_map.64.turned_ref
  23.1 0.0 copy-start.2
  23.1 0.0 collective-permute-done.1.far_ref
  23.1 1.7 %collective-permute-done.near_ref = bf16[4,128,128]{2,1,0:T(8,128)(2,1)S(1)} collective-permute-done((bf16[4,128,128]{2,1,0:T(8,128)(2,1)S(1)}, bf16[4,128,128]{2,1,0:T(8,128)(2,1)S(1)}, u32[]{:S(2)}, u32[]{:S(2)}) %collective-permute-start) | collective-permute-done | bytes 131104 | tf_op jit(solution)/shard_map/ppermute | solution.py:184
  24.8 0.1 broadcast_in_dim.83.meta_ref
  24.9 0.0 copy-done.2
  24.9 2.5 %shard_map.65 = bf16[96,1152]{1,0:T(8,128)(2,1)S(1)} custom-call(s32[4,8]{1,0:T(4,128)S(1)} %copy-done.2, s32[512]{0:T(512)S(1)} %reshape.82.slots_ref, s32[64]{0:T(128)S(1)} %multiply_add_fusion.pos_ref, bf16[96,128]{1,0:T(8,128)(2,1)S(1)} %broadcast_in_dim.83.meta_ref, bf16[4,8,128,128]{3,2,1,0:T(8,128)(2,1)S(1)} %copy-done, ...), custom_call_target="tpu_custom_call" | custom-call | flops 300000000 | bytes 2000000 | tf_op jit(solution)/shard_map/pallas_call | solution.py:118
  27.4 0.1 all_to_all.7
  27.5 19.9 %all_to_all.11 = bf16[48,2,1152]{2,1,0:T(2,128)(2,1)S(1)} all-to-all(bf16[48,2,1152]{2,1,0:T(2,128)(2,1)S(1)} %all_to_all.7), channel_id=1, replica_groups=mesh['grp'=16,'dom'=48] {'dom'}, dimensions={0} | all-to-all | bytes 442368 | tf_op jit(solution)/shard_map/all_to_all | solution.py:198
  47.4 0.1 all_to_all.9.in_ref
  47.5 0.2 shard_map.66
  47.7 20.8 %all_gather.3.in_ref = bf16[256,1024]{1,0:T(8,128)(2,1)S(1)} all-gather(bf16[16,1024]{1,0:T(8,128)(2,1)S(1)} %shard_map.66), channel_id=1, replica_groups=mesh['grp'=16,'dom'=48] {'grp'}, dimensions={0}, use_global_device_ids=true | all-gather | bytes 557056 | tf_op jit(solution)/shard_map/all_gather | solution.py:200
  68.5 1.0 %shard_map.67 = f32[256,1024]{1,0:T(8,128)} custom-call(bf16[256,1024]{1,0:T(8,128)(2,1)S(1)} %all_gather.3.in_ref), custom_call_target="tpu_custom_call" | custom-call | tf_op jit(solution)/shard_map/pallas_call | solution.py:163
  (4 shorter events, 0.0 us)
Async XLA Ops:
  0.0 0.8 %copy-start.4 = (s32[1,8]{1,0:T(1,128)S(1)}, s32[1,8]{1,0:T(1,128)}, u32[]{:S(2)}) copy-start(s32[1,8]{1,0:T(1,128)} %param.9) | copy-start | bytes 100
  0.9 20.1 %copy-start.5 = (s32[64]{0:T(128)S(1)}, s32[64]{0:T(128)}, u32[]{:S(2)}) copy-start(s32[64]{0:T(128)} %param.11) | copy-start | bytes 772
  0.9 20.4 %copy-start.3 = (s32[4,4,8,4]{2,3,1,0:T(4,128)S(1)}, s32[4,4,8,4]{2,3,1,0:T(4,128)}, u32[]{:S(2)}) copy-start(s32[4,4,8,4]{2,3,1,0:T(4,128)} %param.10) | copy-start | bytes 6148
  1.1 20.6 %copy-start.1 = (bf16[4,128,128]{2,1,0:T(8,128)(2,1)S(1)}, bf16[4,128,128]{2,1,0:T(8,128)(2,1)}, u32[]{:S(2)}) copy-start(bf16[4,128,128]{2,1,0:T(8,128)(2,1)} %p_ref.3) | copy-start | bytes 393220
  1.1 22.0 %collective-permute-start.1 = (bf16[4,128,128]{2,1,0:T(8,128)(2,1)S(1)}, bf16[4,128,128]{2,1,0:T(8,128)(2,1)S(1)}, u32[]{:S(2)}, u32[]{:S(2)}) collective-permute-start(bf16[4,128,128]{2,1,0:T(8,128)(2,1)S(1)} %get-tuple-element.9), channel_id=1, source_target_pairs={{1,2},{2,1},{3,4},{4,3},{5,6},{6,5},{7,8},{8,7},{9,10},{10,9},{11,... | collective-permute-start | bytes 393224 | tf_op jit(solution)/shard_map/ppermute | solution.py:183
  19.1 5.7 %collective-permute-start = (bf16[4,128,128]{2,1,0:T(8,128)(2,1)S(1)}, bf16[4,128,128]{2,1,0:T(8,128)(2,1)S(1)}, u32[]{:S(2)}, u32[]{:S(2)}) collective-permute-start(bf16[4,128,128]{2,1,0:T(8,128)(2,1)S(1)} %get-tuple-element.10), channel_id=1, source_target_pairs={{0,1},{1,0},{2,3},{3,2},{4,5},{5,4},{6,7},{7,6},{8,9},{9,8},{10,11... | collective-permute-start | bytes 393224 | tf_op jit(solution)/shard_map/ppermute | solution.py:184
  21.7 1.2 %copy-start = (bf16[4,8,128,128]{3,2,1,0:T(8,128)(2,1)S(1)}, bf16[4,8,128,128]{3,2,1,0:T(8,128)(2,1)}, u32[]{:S(2)}) copy-start(bf16[4,8,128,128]{3,2,1,0:T(8,128)(2,1)} %a_ref.3) | copy-start | bytes 3145732
  23.1 1.8 %copy-start.2 = (s32[4,8]{1,0:T(4,128)S(1)}, s32[4,8]{1,0:T(4,128)}, u32[]{:S(2)}) copy-start(s32[4,8]{1,0:T(4,128)} %cols_ref.1) | copy-start | bytes 388
